TPU v7x, 256 devices: a whole 4x4x8 slice. The times are simulated.
256 devices in a mesh: bus: 16 (over z_hi, x, core), line: 16 (over y, z_lo).
Axes of the slice: x: 4, y: 4, z: 8 (z_hi: 2, z_lo: 4; z = z_hi * 4 + z_lo), core: 2. Of those that a mesh axis runs over, the one named last changes fastest.
Arguments:
- xrows: bfloat16 [2048, 81920], P('line', 'bus')
- inject: bfloat16 [81920, 96], P('bus'), may hold values from -6 to 6
- line_from: int32 [4096], replicated, may hold values from 0 to 2047
- line_to: int32 [4096], replicated, may hold values from 0 to 2047, as said below
- suscept: float32 [4096], P('line'), may hold values from 1 to 4
- rating: float32 [4096], P('line'), may hold values from 1 to 8
- region_bus: int32 [2048], replicated, may hold values from 0 to 81919, as said below
- outage: int32 [1024], replicated, may hold values from 0 to 4095
Outputs:
- loading: float32 [4096, 1024], P('line', 'bus')
- base_flow: float32 [4096, 96], P('line')
Inputs may be any that keep to these rules, and one draw needn't show every extreme that they name: line_to differs from line_from in every line. `region_bus`: all entries differ.
All inputs are finite; a program needn't handle non-finite values.
Results may differ from a plain program's by a relative error of at most 0.0003.
Values may be sent and summed in bfloat16 or wider, within the bound.
A program may use at most 128 MiB of HBM per device.

v0:
```python
import jax
import jax.numpy as jnp
from jax import lax
from jax.sharding import PartitionSpec as P


def sum_buses(partial_value, kcount, kshare):
    totals = lax.psum(partial_value, "bus")
    k_first = lax.axis_index("bus") * kshare
    own_cols = lax.dynamic_slice_in_dim(totals[:, :kcount], k_first, kshare, 1)
    return jnp.concatenate([own_cols, totals[:, kcount:]], axis=1)


def line_difference(values, my_from, my_to):
    count = values.shape[0]
    in_from = (my_from >= 0) & (my_from < count)
    in_to = (my_to >= 0) & (my_to < count)
    upper = jnp.where(
        in_from[:, None], jnp.take(values, jnp.clip(my_from, 0, count - 1), axis=0), 0.0
    )
    lower = jnp.where(in_to[:, None], jnp.take(values, jnp.clip(my_to, 0, count - 1), axis=0), 0.0)
    return upper - lower


def on_device(xrows, inject, line_from, line_to, suscept, rating, region_bus, outage):
    rows_loc, bus_loc = xrows.shape
    lines_loc = suscept.shape[0]
    region = lax.axis_size("line") * rows_loc
    kcount = outage.shape[0]
    kshare = kcount // lax.axis_size("bus")
    line_start = lax.axis_index("line") * lines_loc
    bus_start = lax.axis_index("bus") * bus_loc
    my_from = lax.dynamic_slice_in_dim(line_from, line_start, lines_loc)
    my_to = lax.dynamic_slice_in_dim(line_to, line_start, lines_loc)
    ends_from = region_bus[line_from[outage]] - bus_start
    ends_to = region_bus[line_to[outage]] - bus_start
    inside_from = (ends_from >= 0) & (ends_from < bus_loc)
    inside_to = (ends_to >= 0) & (ends_to < bus_loc)
    col_from = jnp.clip(ends_from, 0, bus_loc - 1)
    col_to = jnp.clip(ends_to, 0, bus_loc - 1)
    region_iota = jnp.arange(region, dtype=jnp.int32)
    incidence = (
        (my_from[:, None] == region_iota[None, :]).astype(jnp.float32)
        - (my_to[:, None] == region_iota[None, :]).astype(jnp.float32)
    ).astype(jnp.bfloat16)
    piece = lax.all_gather(xrows, "line", axis=0, tiled=True)
    diff_total = jnp.dot(incidence, piece, preferred_element_type=jnp.float32)
    spread_piece = jnp.dot(piece, inject, preferred_element_type=jnp.float32)
    flow_total = line_difference(spread_piece, my_from, my_to)
    upper = jnp.where(inside_from[None, :], jnp.take(diff_total, col_from, axis=1), 0.0)
    lower = jnp.where(inside_to[None, :], jnp.take(diff_total, col_to, axis=1), 0.0)
    partial_value = jnp.concatenate([upper - lower, flow_total], axis=1)
    sensitivity = sum_buses(partial_value, kcount, kshare)
    scaled = suscept[:, None] * sensitivity
    lodf_part = scaled[:, :kshare]
    base_flow = scaled[:, kshare:]
    my_outage = lax.dynamic_slice_in_dim(outage, lax.axis_index("bus") * kshare, kshare)
    owner = (
        my_outage[:, None] == line_start + jnp.arange(lines_loc, dtype=jnp.int32)[None, :]
    ).astype(jnp.float32)
    flow_part = jnp.dot(owner, base_flow, precision=lax.Precision.HIGHEST)
    own_part = jnp.sum(owner * lodf_part.T, axis=1)
    outage_flow, own_term = lax.psum((flow_part, own_part), "line")
    divisor = jnp.maximum(1.0 - own_term, 0.25)
    scaled_ratio = lodf_part / divisor[None, :]
    post_flow = base_flow[:, None, :] + scaled_ratio[:, :, None] * outage_flow[None, :, :]
    loading = jnp.max(jnp.abs(post_flow), axis=2) / rating[:, None]
    return (loading, base_flow)


def solution(mesh):
    placed = (P("line", "bus"), P("bus", None), P(), P(), P("line"), P("line"), P(), P())
    return jax.shard_map(
        on_device,
        mesh=mesh,
        in_specs=placed,
        out_specs=(P("line", "bus"), P("line", None)),
        check_vma=False,
    )
```

profile of v0, /device:TPU:1, one launch (start us, length us, event | category | flops | bytes accessed | tf_op | source)
XLA Modules:
  0.0 748.7 jit_solution(12566912486449012320)
XLA Ops:
  7.2 0.0 copy-start
  7.2 0.0 all-gather.2.cloned.1.call-start
  7.2 0.7 all-gather.2.cloned.1.call-update
  7.9 0.0 all-reduce.3.cloned.1.call-start
  8.0 0.7 fusion.10
  8.7 5.7 gather_fusion
  14.4 6.2 gather_fusion.2
  20.6 6.2 gather_fusion.1
  26.8 6.2 gather_fusion.3
  33.0 0.8 compare_and_fusion.6
  33.9 418.4 %all-gather.2.cloned.1.call-done = bf16[2048,5120]{1,0:T(8,128)(2,1)} async-done(((bf16[128,5120]{1,0:T(8,128)(2,1)}), bf16[2048,5120]{1,0:T(8,128)(2,1)}) %all-gather.2.cloned.1.call-update) | async-done | bytes 20971536 | tf_op jit(solution)/shard_map/all_gather | solution.py:46
  452.3 9.8 %fusion.13 = f32[2048,96]{1,0:T(8,128)S(1)} fusion(bf16[2048,5120]{1,0:T(8,128)(2,1)} %all-gather.2.cloned.1.call-done, bf16[5120,96]{0,1:T(8,128)(2,1)S(1)} %copy-done), kind=kOutput, calls=%fused_computation.56 | convolution fusion | flops 2013265920 | bytes 22740992 | tf_op jit(solution)/shard_map/dot_general | solution.py:48
  462.1 0.7 gather_fusion.7
  462.9 0.1 copy.31
  463.0 0.7 gather_fusion.6
  463.7 0.1 copy.29
  463.8 15.0 %fusion = f32[256,5120]{0,1:T(8,128)} fusion(bf16[2048,5120]{1,0:T(8,128)(2,1)} %all-gather.2.cloned.1.call-done, s32[256]{0:T(256)S(1)} %get-tuple-element.9, s32[256]{0:T(256)S(1)} %get-tuple-element.15), kind=kOutput, calls=%fused_computation.13 | convolution fusion | flops 5371854848 | bytes 26216448 | tf_op jit(solution)/shard_map/dot_general | solution.py:47
  478.8 5.9 gather_fusion.5
  484.7 5.9 gather_fusion.4
  490.7 0.9 fusion.1
  491.7 1.1 pad_maximum_fusion
  492.8 0.0 all-reduce.3.cloned.1.call-update
  492.8 0.8 dynamic_slice.15
  493.6 179.9 %all-reduce.3.cloned.1.call-done = f32[256,1120]{0,1:T(8,128)} async-done(((f32[256,1120]{0,1:T(8,128)}), f32[256,1120]{0,1:T(8,128)}) %all-reduce.3.cloned.1.call-update) | async-done | bytes 1146896 | tf_op jit(solution)/shard_map/psum | solution.py:8
  673.4 1.3 slice.32
  674.8 0.9 slice.33
  675.7 0.2 fusion.7
  675.9 0.2 fusion.5
  676.1 63.7 %all-reduce = (f32[64,96]{1,0:T(8,128)S(1)}, f32[64]{0:T(128)S(1)}) all-reduce(f32[64,96]{1,0:T(8,128)S(1)} %fusion.5, f32[64]{0:T(128)S(1)} %fusion.7), channel_id=1, replica_groups=mesh['bus'=16,'line'=16] {'line'}, use_global_device_ids=true, to_apply=%region_3.6 | all-reduce | flops 6208 | bytes 49664 | tf_op jit(solution)/shard_map/psum | solution.py:63
  739.8 0.1 slice_divide_fusion
  739.9 1.2 abs_reduce_fusion
  741.2 0.6 broadcast_divide_fusion
  (29 shorter events, 0.2 us)
Async XLA Ops:
  7.2 445.1 %copy-start = (bf16[5120,96]{0,1:T(8,128)(2,1)S(1)}, bf16[5120,96]{0,1:T(8,128)(2,1)}, u32[]{:S(2)}) copy-start(bf16[5120,96]{0,1:T(8,128)(2,1)} %param.13) | copy-start | bytes 2949124
  7.2 7.3 copy-start.2
  7.2 13.4 %copy-start.1 = (s32[2048]{0:T(1024)S(1)}, s32[2048]{0:T(1024)}, u32[]{:S(2)}) copy-start(s32[2048]{0:T(1024)} %param.18) | copy-start | bytes 24580
  7.2 445.1 %all-gather.2.cloned.1.call-start = ((), (), s32[]{:S(2)}) async-start(), calls=%async_computation | async-start | bytes 22282240 | tf_op jit(solution)/shard_map/all_gather | solution.py:46
  7.9 665.5 %all-reduce.3.cloned.1.call-start = ((), (), s32[]{:S(2)}) async-start(), calls=%async_computation.1 | async-start | bytes 2293760 | tf_op jit(solution)/shard_map/psum | solution.py:8
  490.7 185.0 %copy-start.4 = (f32[256]{0:T(256)S(1)}, f32[256]{0:T(256)}, u32[]{:S(2)}) copy-start(f32[256]{0:T(256)} %param.16) | copy-start | bytes 3076
  490.7 250.5 %copy-start.5 = (f32[256]{0:T(256)S(1)}, f32[256]{0:T(256)}, u32[]{:S(2)}) copy-start(f32[256]{0:T(256)} %param.17) | copy-start | bytes 3076
  675.7 66.1 %copy-start.3 = (f32[256,96]{0,1:T(8,128)}, f32[256,96]{0,1:T(8,128)S(1)}, u32[]{:S(2)}) copy-start(f32[256,96]{0,1:T(8,128)S(1)} %slice.34) | copy-start | bytes 294916
Sparse Core Ops, SparseCore 0:
  9.8 442.4 all-gather.1
  492.9 180.4 all-reduce.2
where the time goes:
time: 762 us; the launch traced here: 749 us
  waiting for transfers between devices  599 us (79%)
  blocking collectives  63.7 us (8%)
  local copies, waits for them, and re-layouts  40.8 us (5%)
  matrix products  25.1 us (3%)
  between operations  14.4 us (2%)
    all_gather x1, waiting for transfers between devices, on_device(): piece = lax.all_gather(xrows, 'line', axis=0, tiled=True)  418 us
    psum x1, waiting for transfers between devices, sum_buses(): totals = lax.psum(partial_value, 'bus')  180 us
    psum x1, blocking collectives, on_device(): outage_flow, own_term = lax.psum((flow_part, own_part), 'line')  63.7 us
  transfers between devices with their start and end apart: 2, of which 2 were waited for; matrix products, arithmetic and copies ran while one was open for 4% of the time, Pallas kernels for 0%

commit v1 on v0

v1 whole, which is shorter than its diff:
```python
import functools

import jax
import jax.numpy as jnp
from jax import lax
from jax.experimental import pallas as pl
from jax.experimental.pallas import tpu as pltpu
from jax.sharding import PartitionSpec as P

MESH = pl.DeviceIdType.MESH
NX, NC, NZH, NY, NZL = 4, 2, 2, 4, 4
HOURS = 12
HPAD = 16
KS = 64
CHUNKS = (32, 32)
OFFS = (0, 32)
WIDTH = (CHUNKS[0] + HPAD, CHUNKS[1])
ROWS = (2 * CHUNKS[0] + HPAD, 2 * CHUNKS[1])


def index_kernel(lines_tiles, bus_loc, outage_ref, from_ref, to_ref, region_ref, out_ref):
    outage = outage_ref[...]
    lo = outage % 128
    hi = outage // 128

    def pick(table_ref, tiles, low, high):
        total = jnp.zeros((8, 128), jnp.int32)
        for t in range(tiles):
            row = jnp.broadcast_to(table_ref[t : t + 1, :], (8, 128))
            got = jnp.take_along_axis(row, low, axis=1, mode="promise_in_bounds")
            total = jnp.where(high == t, got, total)
        return total

    rf = pick(from_ref, 32, lo, hi)
    rt = pick(to_ref, 32, lo, hi)
    start = lax.axis_index("bus") * bus_loc
    ef = pick(region_ref, 16, rf % 128, rf // 128) - start
    et = pick(region_ref, 16, rt % 128, rt // 128) - start
    out_ref[0:8, :] = jnp.where((ef >= 0) & (ef < bus_loc), ef, -512)
    out_ref[8:16, :] = jnp.where((et >= 0) & (et < bus_loc), et, -512)
    out_ref[16:24, :] = rf
    out_ref[24:32, :] = rt
    me = lax.axis_index("line")
    out_ref[32:34, :] = from_ref[pl.ds(me * lines_tiles, lines_tiles), :]
    out_ref[34:36, :] = to_ref[pl.ds(me * lines_tiles, lines_tiles), :]
    out_ref[36:40, :] = jnp.zeros((4, 128), jnp.int32)


def three(v):
    a = v.astype(jnp.bfloat16)
    r = v - a.astype(jnp.float32)
    b = r.astype(jnp.bfloat16)
    c = (r - b.astype(jnp.float32)).astype(jnp.bfloat16)
    return jnp.concatenate([a, b, c], axis=0)


def dot3(parts, rhs, rows):
    d = jnp.dot(parts, rhs, preferred_element_type=jnp.float32)
    return d[0:rows] + d[rows : 2 * rows] + d[2 * rows : 3 * rows]


def main_kernel(
    x_ref, inject_ref, idx_ref, outage_ref, susc2_ref, susc_ref, rating_ref,
    load_ref, base_ref,
    efc, etc, hb, pb0, pb1, ra0, ra1, q0, q1, rb0, rb1, p0, p1, rc0, rc1, full0, full1,
    inc, s4, r4, s0s, s0r, s1s, s1r, s2s, s2r, s3s, s3r, s4s, s4r,
):
    b = lax.axis_index("bus")
    l = lax.axis_index("line")
    zh, x, c = b // 8, (b // 2) % 4, b % 2
    y, zl = l // 4, l % 4
    z = zh * 4 + zl
    bus_loc = x_ref.shape[1]

    def at(zh_, x_, c_, y_, zl_):
        return {"bus": (zh_ * 4 + x_) * 2 + c_, "line": y_ * 4 + zl_}

    group = [((x + dx) % 4, (c + dc) % 2) for dx in range(4) for dc in range(2) if dx or dc]
    zpeers = [(z + dz) % 8 for dz in range(1, 8)]
    zfrom = [(z + 8 - dz) % 8 for dz in range(1, 8)]

    barrier = pltpu.get_barrier_semaphore()
    for gx, gc in group:
        pl.semaphore_signal(barrier, 1, device_id=at(zh, gx, gc, y, zl), device_id_type=MESH)
    for pz in zpeers:
        pl.semaphore_signal(barrier, 1, device_id=at(pz // 4, x, c, y, pz % 4), device_id_type=MESH)
    for dy in range(1, 4):
        pl.semaphore_signal(barrier, 1, device_id=at(zh, x, c, (y + dy) % 4, zl), device_id_type=MESH)

    pb, ra, q, rb, p, rc, full = (pb0, pb1), (ra0, ra1), (q0, q1), (rb0, rb1), (p0, p1), (rc0, rc1), (full0, full1)

    lane = lax.broadcasted_iota(jnp.int32, (128, 128), 1)
    for s in range(8):
        ef = jnp.broadcast_to(idx_ref[s : s + 1, :], (128, 128)).T
        et = jnp.broadcast_to(idx_ref[8 + s : 9 + s, :], (128, 128)).T
        efc[s] = (ef - lane).astype(jnp.int16)
        etc[s] = (et - lane).astype(jnp.int16)

    spread = jnp.dot(x_ref[...], inject_ref[...], preferred_element_type=jnp.float32)
    spread_t = spread.T
    zero4 = jnp.zeros((HPAD - HOURS, 128), jnp.float32)
    for xd in range(4):
        for cd in range(2):
            first = (xd * 2 + cd) * HOURS
            hb[cd, xd] = jnp.concatenate([spread_t[first : first + HOURS], zero4], axis=0)

    one = jnp.bfloat16(1.0)
    minus = jnp.bfloat16(-1.0)
    zero = jnp.bfloat16(0.0)
    step = 1024

    def select(ch, cd):
        k = CHUNKS[ch]
        at_row = pl.multiple_of(cd * 64 + OFFS[ch], 16)
        ef = jnp.concatenate([efc[zd * 4 + xd, pl.ds(at_row, k), :] for xd in range(4) for zd in range(2)], axis=0)
        et = jnp.concatenate([etc[zd * 4 + xd, pl.ds(at_row, k), :] for xd in range(4) for zd in range(2)], axis=0)
        acc = jnp.zeros((8 * k, 128), jnp.float32)
        for t in range(bus_loc // step):
            cols = []
            for u in range(step // 128):
                here = jnp.int16(t * step + u * 128)
                cols.append(jnp.where(ef == here, one, jnp.where(et == here, minus, zero)))
            acc = acc + lax.dot_general(
                jnp.concatenate(cols, axis=1), x_ref[:, t * step : (t + 1) * step],
                (((1,), (1,)), ((), ())), preferred_element_type=jnp.float32,
            )
        for xd in range(4):
            pb[ch][cd, xd, 0 : 2 * k, :] = acc[xd * 2 * k : (xd + 1) * 2 * k]
        if ch == 0:
            for xd in range(4):
                pb[ch][cd, xd, 2 * k : 2 * k + HPAD, :] = hb[cd, xd]

    started = []

    def start(src, dst, ss, rs, where):
        copy = pltpu.make_async_remote_copy(
            src_ref=src, dst_ref=dst, send_sem=ss, recv_sem=rs, device_id=where, device_id_type=MESH
        )
        copy.start()
        started.append(copy)

    def arrived(src, dst, ss, rs):
        pltpu.make_async_remote_copy(
            src_ref=src, dst_ref=dst, send_sem=ss, recv_sem=rs,
            device_id=at(zh, x, 1 - c, y, zl), device_id_type=MESH,
        ).wait_recv()

    def send0(ch):
        start(pb[ch].at[1 - c], ra[ch], s0s.at[ch], s0r.at[ch], at(zh, x, 1 - c, y, zl))

    def send1(ch):
        arrived(pb[ch].at[1 - c], ra[ch], s0s.at[ch], s0r.at[ch])
        q[ch][...] = pb[ch][c] + ra[ch][...]
        for dx in (2, 1, 3):
            px = (x + dx) % 4
            start(q[ch].at[px], rb[ch].at[x], s1s.at[ch, dx], s1r.at[ch, dx], at(zh, px, c, y, zl))

    def send2(ch):
        k = CHUNKS[ch]
        rb[ch][x] = q[ch][x]
        for dx in (1, 3, 2):
            fx = (x + 4 - dx) % 4
            arrived(q[ch].at[fx], rb[ch].at[fx], s1s.at[ch, dx], s1r.at[ch, dx])
        total = (rb[ch][0] + rb[ch][1]) + (rb[ch][2] + rb[ch][3])
        for zd in range(2):
            p[ch][zd, 0:k, :] = total[zd * k : (zd + 1) * k]
        if ch == 0:
            mine = jnp.where(zh == 0, 1.0, 0.0) * susc2_ref[...]
            tail = jnp.concatenate(
                [total[2 * k : 2 * k + HOURS], mine, jnp.zeros((2, 128), jnp.float32)], axis=0
            )
            for zd in range(2):
                p[ch][zd, k : k + HPAD, :] = tail
        for dz in (4, 3, 5, 2, 6, 1, 7):
            pz = (z + dz) % 8
            start(p[ch].at[pz // 4], rc[ch].at[z], s2s.at[ch, dz], s2r.at[ch, dz], at(pz // 4, x, c, y, pz % 4))

    def send3(ch):
        rc[ch][z] = p[ch][zh]
        for dz in (1, 7, 2, 6, 3, 5, 4):
            fz = (z + 8 - dz) % 8
            arrived(p[ch].at[0], rc[ch].at[fz], s2s.at[ch, dz], s2r.at[ch, dz])
        full[ch][y] = rc[ch][0:4] + rc[ch][4:8]
        for dy in (2, 1, 3):
            py = (y + dy) % 4
            start(full[ch].at[y], full[ch].at[y], s3s.at[ch, dy], s3r.at[ch, dy], at(zh, x, c, py, zl))

    def gathered(ch):
        for dy in (1, 3, 2):
            fy = (y + 4 - dy) % 4
            arrived(full[ch].at[y], full[ch].at[fy], s3s.at[ch, dy], s3r.at[ch, dy])

    select(0, 1 - c)
    pl.semaphore_wait(barrier, 17)
    send0(0)
    select(0, c)
    send1(0)
    select(1, 1 - c)
    send0(1)
    select(1, c)
    send1(1)

    for g in range(6):
        if g < 2:
            rf = idx_ref[32 + g : 33 + g, :]
            rt = idx_ref[34 + g : 35 + g, :]
        else:
            rf = idx_ref[pl.ds(16 + zh * 4 + g - 2, 1), :]
            rt = idx_ref[pl.ds(24 + zh * 4 + g - 2, 1), :]
        sub = lax.broadcasted_iota(jnp.int32, (128, 128), 0)
        f16 = (jnp.broadcast_to(rf, (128, 128)) - sub).astype(jnp.int16)
        t16 = (jnp.broadcast_to(rt, (128, 128)) - sub).astype(jnp.int16)
        for r in range(16):
            here = jnp.int16(r * 128)
            inc[r * 128 : (r + 1) * 128, g * 128 : (g + 1) * 128] = jnp.where(
                f16 == here, one, jnp.where(t16 == here, minus, zero)
            )

    send2(0)
    send2(1)
    send3(0)
    send3(1)

    k0 = CHUNKS[0]
    gathered(0)
    hours = jnp.concatenate([full0[i // 4, i % 4, k0 : k0 + HPAD, :] for i in range(16)], axis=1)
    flows = dot3(three(hours), inc[...], HPAD)
    own_flow = flows[:, 0:256] * susc_ref[...]
    for xd in range(4):
        s4[xd, :, 0:256] = own_flow
        s4[xd, :, 256:384] = flows[:, 256 + xd * 128 : 384 + xd * 128]
    for i, (gx, gc) in enumerate(group):
        start(s4.at[gx], r4.at[x * 2 + c], s4s.at[i], s4r.at[i], at(zh, gx, gc, y, zl))
    r4[x * 2 + c] = s4[x]

    row = outage_ref[pl.ds(zh * 4 + x, 1), :]
    table = jnp.concatenate([full0[i // 4, i % 4, k0 + HOURS : k0 + HOURS + 2, :] for i in range(16)], axis=0)
    low = jnp.broadcast_to(row % 128, (128, 128))
    hot = jnp.where(low == lax.broadcasted_iota(jnp.int32, (128, 128), 0), 1.0, 0.0).astype(jnp.bfloat16)
    cand = dot3(three(table), hot, 32)
    high = jnp.broadcast_to(row // 128, (32, 128))
    susc_out = jnp.sum(
        jnp.where(high == lax.broadcasted_iota(jnp.int32, (32, 128), 0), cand, 0.0), axis=0, keepdims=True
    )

    own_inc = inc[:, pl.ds(pl.multiple_of(256 + x * 128, 128), 128)]
    sens, diag = [], []
    for ch in range(2):
        if ch == 1:
            gathered(1)
        k = CHUNKS[ch]
        shifted = three(jnp.concatenate([full[ch][i // 4, i % 4, 0:k, :] for i in range(16)], axis=1))
        sens.append(dot3(shifted, inc[:, 0:256], k))
        diag.append(dot3(shifted, own_inc, k))
    sens = jnp.concatenate(sens, axis=0) * susc_ref[...]
    diag = jnp.concatenate(diag, axis=0) * susc_out
    here = lax.broadcasted_iota(jnp.int32, (KS, 128), 1) == lax.broadcasted_iota(jnp.int32, (KS, 128), 0) + c * KS
    own = jnp.sum(jnp.where(here, diag, 0.0), axis=1, keepdims=True)
    ratio = sens / jnp.maximum(1.0 - own, 0.25)

    for i, (gx, gc) in enumerate(group):
        fx, fc = (x + 4 - (i + 1) // 2) % 4, (c + (i + 1) % 2) % 2
        arrived(s4.at[0], r4.at[fx * 2 + fc], s4s.at[i], s4r.at[i])

    outflow = r4[:, :, 256:384].reshape(128, 128) * susc_out
    outflow = outflow.T
    outflow = jnp.where(c == 0, outflow[0:KS], outflow[KS : 2 * KS])
    worst = jnp.zeros((KS, 256), jnp.float32)
    for s in range(8):
        for h in range(HOURS):
            flow = r4[s, h : h + 1, 0:256]
            col = outflow[:, s * HPAD + h : s * HPAD + h + 1]
            worst = jnp.maximum(worst, jnp.abs(flow + ratio * col))
    load_ref[...] = worst / rating_ref[...]
    for s in range(8):
        base_ref[s * HOURS : (s + 1) * HOURS, :] = r4[s, 0:HOURS, 0:256]

    for copy in started:
        copy.wait_send()


def on_device(xrows, inject, line_from, line_to, suscept, rating, region_bus, outage):
    bus_loc = xrows.shape[1]
    vm = pl.BlockSpec(memory_space=pltpu.VMEM)
    out8 = outage.reshape(8, 128)
    idx = pl.pallas_call(
        functools.partial(index_kernel, 2, bus_loc),
        out_shape=jax.ShapeDtypeStruct((40, 128), jnp.int32),
        in_specs=[vm] * 4,
        out_specs=vm,
        name="indices",
    )(out8, line_from.reshape(32, 128), line_to.reshape(32, 128), region_bus.reshape(16, 128))
    f32, bf16, i16 = jnp.float32, jnp.bfloat16, jnp.int16
    both = lambda lead, counts, kind=f32: [pltpu.VMEM(lead + (n, 128), kind) for n in counts]
    load_t, base_t = pl.pallas_call(
        main_kernel,
        out_shape=(jax.ShapeDtypeStruct((KS, 256), f32), jax.ShapeDtypeStruct((96, 256), f32)),
        in_specs=[vm] * 7,
        out_specs=(vm, vm),
        scratch_shapes=[
            pltpu.VMEM((8, 128, 128), i16),
            pltpu.VMEM((8, 128, 128), i16),
            pltpu.VMEM((2, 4, HPAD, 128), f32),
            *both((2, 4), ROWS),
            *both((4,), ROWS),
            *both((4,), ROWS),
            *both((4,), ROWS),
            *both((2,), WIDTH),
            *both((8,), WIDTH),
            *both((4, 4), WIDTH),
            pltpu.VMEM((2048, 768), bf16),
            pltpu.VMEM((4, HPAD, 384), f32),
            pltpu.VMEM((8, HPAD, 384), f32),
            pltpu.SemaphoreType.DMA((2,)),
            pltpu.SemaphoreType.DMA((2,)),
            pltpu.SemaphoreType.DMA((2, 4)),
            pltpu.SemaphoreType.DMA((2, 4)),
            pltpu.SemaphoreType.DMA((2, 8)),
            pltpu.SemaphoreType.DMA((2, 8)),
            pltpu.SemaphoreType.DMA((2, 4)),
            pltpu.SemaphoreType.DMA((2, 4)),
            pltpu.SemaphoreType.DMA((7,)),
            pltpu.SemaphoreType.DMA((7,)),
        ],
        compiler_params=pltpu.CompilerParams(
            collective_id=0, has_side_effects=True, vmem_limit_bytes=48 * 1024 * 1024
        ),
        name="exchange",
    )(xrows, inject, idx, out8, suscept.reshape(2, 128), suscept.reshape(1, 256), rating.reshape(1, 256))
    return load_t.T, base_t.T


def solution(mesh):
    placed = (P("line", "bus"), P("bus", None), P(), P(), P("line"), P("line"), P(), P())
    return jax.shard_map(
        on_device,
        mesh=mesh,
        in_specs=placed,
        out_specs=(P("line", "bus"), P("line", None)),
        check_vma=False,
    )
```

time: 762 us -> 42.7 us (0.06); the launches traced: 749 us -> 42.6 us
  waiting for transfers between devices: 599 us -> 0 us
  blocking collectives: 63.7 us -> 0 us
  Pallas kernels: 0 us -> 38.9 us
  local copies, waits for them, and re-layouts: 40.8 us -> 3.01 us
  matrix products: 25.1 us -> 0 us
  between operations: 14.4 us -> 0.72 us
    all_gather x1 -> x0, waiting for transfers between devices: 418 us -> none  [on_device(): piece = lax.all_gather(xrows, 'line', axis=0, tiled=True)]
    psum x1 -> x0, waiting for transfers between devices: 180 us -> none  [sum_buses(): totals = lax.psum(partial_value, 'bus')]
    psum x1 -> x0, blocking collectives: 63.7 us -> none  [on_device(): outage_flow, own_term = lax.psum((flow_part, own_part), 'line')]
    pallas_call x0 -> x2, Pallas kernels: none -> 38.9 us  [the longest x1 37.1 us: on_device(): pl.pallas_call(main_kernel, out_shape=(jax.ShapeDtypeStruct((KS, 256), f3...]
    gather x10 -> x0, local copies, waits for them, and re-layouts: 37.7 us -> none  [the longest x2 12.3 us: on_device(): ends_to = region_bus[line_to[outage]] - bus_start]
    dot_general x3 -> x0, matrix products: 25.1 us -> none  [the longest x1 15 us: on_device(): diff_total = jnp.dot(incidence, piece, preferred_element_type=jnp.float32)]
  transfers between devices with their start and end apart: 2 -> 0, of which waited for: 2 -> 0; matrix products, arithmetic and copies ran while one was open for 4% -> 0% of each run, Pallas kernels for 0% -> 0%
where the time goes in v1:
time: 42.7 us; the launch traced here: 42.6 us
  Pallas kernels  38.9 us (91%)
  local copies, waits for them, and re-layouts  3.01 us (7%)
  between operations  0.72 us (2%)
    pallas_call x1, Pallas kernels, on_device(): pl.pallas_call(main_kernel, out_shape=(jax.ShapeDtypeStruct((KS, 256), f3...  37.1 us
    unnamed x13, local copies, waits for them, and re-layouts  3.01 us
    pallas_call x1, Pallas kernels, on_device(): pl.pallas_call(functools.partial(index_kernel, 2, bus_loc), out_shape=jax...  1.72 us

profile of v1, /device:TPU:1, one launch (start us, length us, event | category | flops | bytes accessed | tf_op | source)
XLA Modules:
  0.0 42.6 jit_solution(14794012333231293050)
XLA Ops:
  0.6 0.0 copy-start.3
  0.6 0.0 copy-start.2
  0.7 0.0 copy-start.4
  0.7 0.0 copy-start
  0.7 1.7 %indices.1.idx_ref = s32[40,128]{1,0:T(8,128)} custom-call(s32[8,128]{1,0:T(8,128)} %bitcast.11, s32[32,128]{1,0:T(8,128)} %bitcast.16, s32[32,128]{1,0:T(8,128)} %bitcast.17, s32[16,128]{1,0:T(8,128)} %bitcast.18), custom_call_target="tpu_custom_call" | custom-call | tf_op jit(solution)/shard_map/indices/pallas_call | solution.py:286
  2.4 0.0 copy-start.1
  2.4 1.7 %copy.10.inject_ref = bf16[5120,96]{1,0:T(8,128)(2,1)S(1)} copy(bf16[5120,96]{0,1:T(8,128)(2,1)} %param.9) | data formatting | bytes 1966080 | tf_op args[1]
  4.1 0.0 copy-done.3
  4.1 0.0 copy-done.2
  4.1 0.0 copy-done.4
  4.2 0.0 copy-done
  4.2 0.0 copy-done.1
  4.2 37.1 %exchange.1 = (f32[64,256]{1,0:T(8,128)S(1)}, f32[96,256]{1,0:T(8,128)S(1)}) custom-call(bf16[128,5120]{1,0:T(8,128)(2,1)S(1)} %copy-done, bf16[5120,96]{1,0:T(8,128)(2,1)S(1)} %copy.10.inject_ref, s32[40,128]{1,0:T(8,128)S(1)} %copy-done.1, s32[8,128]{1,0:T(8,128)S(1)} %bitcast.12, f32[2,128]{1,0:T(2,128)S(1)} %bitcast.13, f32[1,256]{1,0:T(1,128)S(1)} %bitcast.14, ...), custom_call_target="tpu_custom_call" | custom-call | tf_op jit(solution)/shard_map/exchange/pallas_call | solution.py:295
  41.3 0.6 %copy.13 = f32[256,64]{0,1:T(8,128)} copy(f32[256,64]{0,1:T(8,128)S(1)} %bitcast.10) | data formatting | bytes 131072
  41.9 0.6 %copy.14 = f32[256,96]{0,1:T(8,128)} copy(f32[256,96]{0,1:T(8,128)S(1)} %bitcast.9) | data formatting | bytes 196608
Async XLA Ops:
  0.6 3.5 %copy-start.3 = (f32[256]{0:T(256)S(1)}, f32[256]{0:T(256)}, u32[]{:S(2)}) copy-start(f32[256]{0:T(256)} %param.12) | copy-start | bytes 3076
  0.6 3.5 %copy-start.2 = (s32[1024]{0:T(1024)S(1)}, s32[1024]{0:T(1024)}, u32[]{:S(2)}) copy-start(s32[1024]{0:T(1024)} %param.15) | copy-start | bytes 12292
  0.7 3.5 %copy-start.4 = (f32[256]{0:T(256)S(1)}, f32[256]{0:T(256)}, u32[]{:S(2)}) copy-start(f32[256]{0:T(256)} %param.13) | copy-start | bytes 3076
  0.7 3.5 %copy-start = (bf16[128,5120]{1,0:T(8,128)(2,1)S(1)}, bf16[128,5120]{1,0:T(8,128)(2,1)}, u32[]{:S(2)}) copy-start(bf16[128,5120]{1,0:T(8,128)(2,1)} %x_ref.1) | copy-start | bytes 3932164
  2.4 1.8 %copy-start.1 = (s32[40,128]{1,0:T(8,128)S(1)}, s32[40,128]{1,0:T(8,128)}, u32[]{:S(2)}) copy-start(s32[40,128]{1,0:T(8,128)} %indices.1.idx_ref) | copy-start | bytes 61444

commit v2 on v1

v2 whole, which is shorter than its diff:
```python
import jax
import jax.numpy as jnp
from jax import lax
from jax.experimental import pallas as pl
from jax.experimental.pallas import tpu as pltpu
from jax.sharding import PartitionSpec as P

MESH = pl.DeviceIdType.MESH
HOURS = 12
HPAD = 16
KS = 64
CHUNKS = (16, 48)
OFFS = tuple(sum(CHUNKS[:i]) for i in range(len(CHUNKS)))
WIDTH = tuple(k + (HPAD if i == 0 else 0) for i, k in enumerate(CHUNKS))
ROWS = tuple(2 * k + (HPAD if i == 0 else 0) for i, k in enumerate(CHUNKS))
NCH = len(CHUNKS)


def three(v):
    a = v.astype(jnp.bfloat16)
    r = v - a.astype(jnp.float32)
    b = r.astype(jnp.bfloat16)
    c = (r - b.astype(jnp.float32)).astype(jnp.bfloat16)
    return jnp.concatenate([a, b, c], axis=0)


def dot3(parts, rhs, rows):
    d = jnp.dot(parts, rhs, preferred_element_type=jnp.float32)
    return d[0:rows] + d[rows : 2 * rows] + d[2 * rows : 3 * rows]


def lookup(table_ref, tiles, index):
    low, high = index & 127, index >> 7
    total = jnp.zeros((8, 128), jnp.int32)
    for t in range(tiles):
        row = jnp.broadcast_to(table_ref[t : t + 1, :], (8, 128))
        got = jnp.take_along_axis(row, low, axis=1, mode="promise_in_bounds")
        total = jnp.where(high == t, got, total)
    return total


def main_kernel(
    x_hbm, inject_hbm, outage_hbm, from_hbm, to_hbm, region_hbm, susc_hbm, rating_hbm,
    load_ref, base_ref,
    x_ref, inject_ref, outage_ref, from_ref, to_ref, region_ref, susc_ref, rating_ref, in_sem,
    ends, efc, etc, hb, pb, ra, q, rb, p, rc, hfull, sp, rs, inc_flow, inc_sens, s4, r4,
    s0s, s0r, s1s, s1r, s2s, s2r, s3s, s3r, shs, shr, s4s, s4r,
):
    b = lax.axis_index("bus")
    l = lax.axis_index("line")
    zh, x, c = b // 8, (b // 2) % 4, b % 2
    y, zl = l // 4, l % 4
    z = zh * 4 + zl
    bus_loc = x_ref.shape[1]

    loads = [
        pltpu.make_async_copy(src, dst, in_sem.at[i])
        for i, (src, dst) in enumerate((
            (outage_hbm, outage_ref), (from_hbm, from_ref), (to_hbm, to_ref), (region_hbm, region_ref),
            (x_hbm, x_ref), (inject_hbm, inject_ref), (susc_hbm, susc_ref), (rating_hbm, rating_ref),
        ))
    ]
    for load in loads:
        load.start()

    def at(zh_, x_, c_, y_, zl_):
        return {"bus": (zh_ * 4 + x_) * 2 + c_, "line": y_ * 4 + zl_}

    group = [((x + dx) % 4, (c + dc) % 2) for dx in range(4) for dc in range(2) if dx or dc]

    barrier = pltpu.get_barrier_semaphore()
    for dz in range(1, 8):
        pz = (z + dz) % 8
        pl.semaphore_signal(barrier, 1, device_id=at(pz // 4, x, c, y, pz % 4), device_id_type=MESH)
    for gx, gc in group:
        pl.semaphore_signal(barrier, 1, device_id=at(zh, gx, gc, y, zl), device_id_type=MESH)
    for dy in range(1, 4):
        pl.semaphore_signal(barrier, 1, device_id=at(zh, x, c, (y + dy) % 4, zl), device_id_type=MESH)

    for load in loads[:4]:
        load.wait()
    rf = lookup(from_ref, 32, outage_ref[...])
    rt = lookup(to_ref, 32, outage_ref[...])
    ends[0] = rf
    ends[1] = rt
    bus_from = lookup(region_ref, 16, rf) - b * bus_loc
    bus_to = lookup(region_ref, 16, rt) - b * bus_loc
    bus_from = jnp.where((bus_from >= 0) & (bus_from < bus_loc), bus_from, -512)
    bus_to = jnp.where((bus_to >= 0) & (bus_to < bus_loc), bus_to, -512)

    lane = lax.broadcasted_iota(jnp.int32, (128, 128), 1)
    for s in range(8):
        efc[s] = (jnp.broadcast_to(bus_from[s : s + 1, :], (128, 128)).T - lane).astype(jnp.int16)
        etc[s] = (jnp.broadcast_to(bus_to[s : s + 1, :], (128, 128)).T - lane).astype(jnp.int16)

    for load in loads[4:]:
        load.wait()
    spread = lax.dot_general(
        inject_ref[...], x_ref[...], (((1,), (1,)), ((), ())), preferred_element_type=jnp.float32
    )
    zero4 = jnp.zeros((HPAD - HOURS, 128), jnp.float32)
    for xd in range(4):
        for cd in range(2):
            first = (xd * 2 + cd) * HOURS
            hb[cd, xd] = jnp.concatenate([spread[first : first + HOURS], zero4], axis=0)

    one = jnp.bfloat16(1.0)
    minus = jnp.bfloat16(-1.0)
    zero = jnp.bfloat16(0.0)
    step = 1024

    def select(ch, cd):
        k = CHUNKS[ch]
        at_row = pl.multiple_of(cd * 64 + OFFS[ch], 16)
        ef = jnp.concatenate([efc[zd * 4 + xd, pl.ds(at_row, k), :] for xd in range(4) for zd in range(2)], axis=0)
        et = jnp.concatenate([etc[zd * 4 + xd, pl.ds(at_row, k), :] for xd in range(4) for zd in range(2)], axis=0)
        acc = jnp.zeros((8 * k, 128), jnp.float32)
        for t in range(bus_loc // step):
            cols = []
            for u in range(step // 128):
                here = jnp.int16(t * step + u * 128)
                cols.append(jnp.where(ef == here, one, jnp.where(et == here, minus, zero)))
            acc = acc + lax.dot_general(
                jnp.concatenate(cols, axis=1), x_ref[:, t * step : (t + 1) * step],
                (((1,), (1,)), ((), ())), preferred_element_type=jnp.float32,
            )
        for xd in range(4):
            pb[ch][cd, xd, 0 : 2 * k, :] = acc[xd * 2 * k : (xd + 1) * 2 * k]
        if ch == 0:
            for xd in range(4):
                pb[ch][cd, xd, 2 * k : 2 * k + HPAD, :] = hb[cd, xd]

    started = []

    def start(src, dst, ss, rs_, where):
        copy = pltpu.make_async_remote_copy(
            src_ref=src, dst_ref=dst, send_sem=ss, recv_sem=rs_, device_id=where, device_id_type=MESH
        )
        copy.start()
        started.append(copy)

    def arrived(src, dst, ss, rs_):
        pltpu.make_async_remote_copy(
            src_ref=src, dst_ref=dst, send_sem=ss, recv_sem=rs_,
            device_id=at(zh, x, 1 - c, y, zl), device_id_type=MESH,
        ).wait_recv()

    def send0(ch):
        start(pb[ch].at[1 - c], ra[ch], s0s.at[ch], s0r.at[ch], at(zh, x, 1 - c, y, zl))

    def send1(ch):
        arrived(pb[ch].at[1 - c], ra[ch], s0s.at[ch], s0r.at[ch])
        q[ch][...] = pb[ch][c] + ra[ch][...]
        for dx in (2, 1, 3):
            px = (x + dx) % 4
            start(q[ch].at[px], rb[ch].at[x], s1s.at[ch, dx], s1r.at[ch, dx], at(zh, px, c, y, zl))

    def send2(ch):
        k = CHUNKS[ch]
        rb[ch][x] = q[ch][x]
        for dx in (1, 3, 2):
            fx = (x + 4 - dx) % 4
            arrived(q[ch].at[fx], rb[ch].at[fx], s1s.at[ch, dx], s1r.at[ch, dx])
        total = (rb[ch][0] + rb[ch][1]) + (rb[ch][2] + rb[ch][3])
        for zd in range(2):
            p[ch][zd, 0:k, :] = total[zd * k : (zd + 1) * k]
        if ch == 0:
            mine = jnp.where(zh == 0, 1.0, 0.0) * susc_ref[...]
            tail = jnp.concatenate(
                [total[2 * k : 2 * k + HOURS], mine, jnp.zeros((2, 128), jnp.float32)], axis=0
            )
            for zd in range(2):
                p[ch][zd, k : k + HPAD, :] = tail
        for dz in (4, 3, 5, 2, 6, 1, 7):
            pz = (z + dz) % 8
            start(p[ch].at[pz // 4], rc[ch].at[z], s2s.at[ch, dz], s2r.at[ch, dz], at(pz // 4, x, c, y, pz % 4))

    def send3(ch):
        k = CHUNKS[ch]
        rc[ch][z] = p[ch][zh]
        for dz in (1, 7, 2, 6, 3, 5, 4):
            fz = (z + 8 - dz) % 8
            arrived(p[ch].at[0], rc[ch].at[fz], s2s.at[ch, dz], s2r.at[ch, dz])
        if ch == 0:
            hfull[y] = rc[ch][0:4, k : k + HPAD, :] + rc[ch][4:8, k : k + HPAD, :]
            for dy in (2, 1, 3):
                py = (y + dy) % 4
                start(hfull.at[y], hfull.at[y], shs.at[dy], shr.at[dy], at(zh, x, c, py, zl))
        rows = three(jnp.concatenate([rc[ch][i, 0:k, :] + rc[ch][4 + i, 0:k, :] for i in range(4)], axis=1))
        part = dot3(rows, inc_sens[...], k)
        for py in range(4):
            sp[ch][py, 0:k, :] = part[:, py * 256 : (py + 1) * 256]
        diag = (
            lax.broadcasted_iota(jnp.int32, (k, 128), 1)
            == lax.broadcasted_iota(jnp.int32, (k, 128), 0) + (c * KS + OFFS[ch])
        )
        own = jnp.sum(jnp.where(diag, part[:, 1024:1152], 0.0), axis=0, keepdims=True)
        own = jnp.broadcast_to(jnp.concatenate([own, own], axis=1), (8, 256))
        for py in range(4):
            sp[ch][py, k : k + 8, :] = own
        for dy in (2, 1, 3):
            py = (y + dy) % 4
            start(sp[ch].at[py], rs[ch].at[y], s3s.at[ch, dy], s3r.at[ch, dy], at(zh, x, c, py, zl))
        rs[ch][y] = sp[ch][y]

    def hot(from_row, to_row, first):
        sub = lax.broadcasted_iota(jnp.int32, (128, 128), 0) + first
        return (
            (jnp.broadcast_to(from_row, (128, 128)) - sub).astype(jnp.int16),
            (jnp.broadcast_to(to_row, (128, 128)) - sub).astype(jnp.int16),
        )

    def fill(out, g, tiles, from_row, to_row, first):
        f16, t16 = hot(from_row, to_row, first)
        for r in range(tiles):
            here = jnp.int16(r * 128)
            out[r * 128 : (r + 1) * 128, g * 128 : (g + 1) * 128] = jnp.where(
                f16 == here, one, jnp.where(t16 == here, minus, zero)
            )

    select(0, 1 - c)
    pl.semaphore_wait(barrier, 17)
    send0(0)
    select(0, c)
    send1(0)
    for ch in range(1, NCH):
        select(ch, 1 - c)
        send0(ch)
        select(ch, c)
        send1(ch)

    for g in range(8):
        at_line = (g // 2 * 4 + zl) * 2 + g % 2
        fill(inc_sens, g, 4, from_ref[pl.ds(at_line, 1), :], to_ref[pl.ds(at_line, 1), :], y * 512)
    at_tile = zh * 4 + x
    fill(inc_sens, 8, 4, ends[0, pl.ds(at_tile, 1), :], ends[1, pl.ds(at_tile, 1), :], y * 512)
    send2(0)
    for g in range(2):
        fill(inc_flow, g, 16, from_ref[pl.ds(l * 2 + g, 1), :], to_ref[pl.ds(l * 2 + g, 1), :], 0)
    for g in range(4):
        fill(inc_flow, 2 + g, 16, ends[0, pl.ds(zh * 4 + g, 1), :], ends[1, pl.ds(zh * 4 + g, 1), :], 0)
    for ch in range(1, NCH):
        send2(ch)
    for ch in range(NCH):
        send3(ch)

    susc_row = jnp.concatenate([susc_ref[0:1, :], susc_ref[1:2, :]], axis=1)
    for dy in (1, 3, 2):
        fy = (y + 4 - dy) % 4
        arrived(hfull.at[y], hfull.at[fy], shs.at[dy], shr.at[dy])
    hours = jnp.concatenate([hfull[i // 4, i % 4] for i in range(16)], axis=1)
    flows = dot3(three(hours), inc_flow[...], HPAD)
    own_flow = flows[:, 0:256] * susc_row
    for xd in range(4):
        s4[xd, :, 0:256] = own_flow
        s4[xd, :, 256:384] = flows[:, 256 + xd * 128 : 384 + xd * 128]
    for i, (gx, gc) in enumerate(group):
        start(s4.at[gx], r4.at[x * 2 + c], s4s.at[i], s4r.at[i], at(zh, gx, gc, y, zl))
    r4[x * 2 + c] = s4[x]

    row = outage_ref[pl.ds(at_tile, 1), :]
    table = jnp.concatenate([hfull[i // 4, i % 4, HOURS : HOURS + 2, :] for i in range(16)], axis=0)
    low = jnp.broadcast_to(row & 127, (128, 128))
    hit = jnp.where(low == lax.broadcasted_iota(jnp.int32, (128, 128), 0), 1.0, 0.0).astype(jnp.bfloat16)
    cand = dot3(three(table), hit, 32)
    high = jnp.broadcast_to(row >> 7, (32, 128))
    susc_out = jnp.sum(
        jnp.where(high == lax.broadcasted_iota(jnp.int32, (32, 128), 0), cand, 0.0), axis=0, keepdims=True
    )

    sens = []
    own = jnp.zeros((1, 128), jnp.float32)
    for ch in range(NCH):
        k = CHUNKS[ch]
        for dy in (1, 3, 2):
            fy = (y + 4 - dy) % 4
            arrived(sp[ch].at[0], rs[ch].at[fy], s3s.at[ch, dy], s3r.at[ch, dy])
        total = (rs[ch][0] + rs[ch][1]) + (rs[ch][2] + rs[ch][3])
        sens.append(total[0:k])
        own = own + total[k : k + 1, 0:128]
    sens = jnp.concatenate(sens, axis=0) * susc_row
    here = lax.broadcasted_iota(jnp.int32, (KS, 128), 1) == lax.broadcasted_iota(jnp.int32, (KS, 128), 0) + c * KS
    divisor = jnp.maximum(1.0 - own * susc_out, 0.25)
    divisor = jnp.sum(jnp.where(here, jnp.broadcast_to(divisor, (KS, 128)), 0.0), axis=1, keepdims=True)
    ratio = sens / divisor

    for i in range(7):
        fx, fc = (x + 4 - (i + 1) // 2) % 4, (c + (i + 1) % 2) % 2
        arrived(s4.at[0], r4.at[fx * 2 + fc], s4s.at[i], s4r.at[i])

    outflow = r4[:, :, 256:384].reshape(128, 128) * susc_out
    outflow = outflow.T
    outflow = jnp.where(c == 0, outflow[0:KS], outflow[KS : 2 * KS])
    worst = jnp.zeros((KS, 256), jnp.float32)
    for s in range(8):
        for h in range(HOURS):
            flow = r4[s, h : h + 1, 0:256]
            col = outflow[:, s * HPAD + h : s * HPAD + h + 1]
            worst = jnp.maximum(worst, jnp.abs(flow + ratio * col))
    load_ref[...] = worst / jnp.concatenate([rating_ref[0:1, :], rating_ref[1:2, :]], axis=1)
    for s in range(8):
        base_ref[s * HOURS : (s + 1) * HOURS, :] = r4[s, 0:HOURS, 0:256]

    for copy in started:
        copy.wait_send()


def on_device(xrows, inject, line_from, line_to, suscept, rating, region_bus, outage):
    vm = pl.BlockSpec(memory_space=pltpu.VMEM)
    far = pl.BlockSpec(memory_space=pl.ANY)
    f32, bf16, i16, i32 = jnp.float32, jnp.bfloat16, jnp.int16, jnp.int32
    vmem = lambda shape, kind=f32: pltpu.VMEM(shape, kind)
    each = lambda lead, counts, last=128: tuple(pltpu.VMEM(lead + (n, last), f32) for n in counts)
    sems = lambda *shape: pltpu.SemaphoreType.DMA(shape)
    args = (
        xrows, inject.T, outage.reshape(8, 128), line_from.reshape(32, 128), line_to.reshape(32, 128),
        region_bus.reshape(16, 128), suscept.reshape(2, 128), rating.reshape(2, 128),
    )
    sens_rows = tuple(k + 8 for k in CHUNKS)
    load_t, base_t = pl.pallas_call(
        main_kernel,
        out_shape=(jax.ShapeDtypeStruct((KS, 256), f32), jax.ShapeDtypeStruct((96, 256), f32)),
        in_specs=[far] * 8,
        out_specs=(vm, vm),
        scratch_shapes=[
            *[vmem(a.shape, a.dtype) for a in args],
            sems(8),
            vmem((2, 8, 128), i32),
            vmem((8, 128, 128), i16),
            vmem((8, 128, 128), i16),
            vmem((2, 4, HPAD, 128)),
            each((2, 4), ROWS),
            each((4,), ROWS),
            each((4,), ROWS),
            each((4,), ROWS),
            each((2,), WIDTH),
            each((8,), WIDTH),
            vmem((4, 4, HPAD, 128)),
            each((4,), sens_rows, 256),
            each((4,), sens_rows, 256),
            vmem((2048, 768), bf16),
            vmem((512, 1152), bf16),
            vmem((4, HPAD, 384)),
            vmem((8, HPAD, 384)),
            sems(NCH), sems(NCH),
            sems(NCH, 4), sems(NCH, 4),
            sems(NCH, 8), sems(NCH, 8),
            sems(NCH, 4), sems(NCH, 4),
            sems(4), sems(4),
            sems(7), sems(7),
        ],
        compiler_params=pltpu.CompilerParams(
            collective_id=0, has_side_effects=True, vmem_limit_bytes=60 * 1024 * 1024
        ),
        name="exchange",
    )(*args)
    return load_t.T, base_t.T


def solution(mesh):
    placed = (P("line", "bus"), P("bus", None), P(), P(), P("line"), P("line"), P(), P())
    return jax.shard_map(
        on_device,
        mesh=mesh,
        in_specs=placed,
        out_specs=(P("line", "bus"), P("line", None)),
        check_vma=False,
    )
```

time: 42.7 us -> 38.7 us (0.906)
  Pallas kernels: 38.9 us -> 34.8 us
    pallas_call x1, Pallas kernels: 37.1 us -> 34.8 us  [on_device(): pl.pallas_call(main_kernel, out_shape=(jax.ShapeDtypeStruct((KS, 256), f3...]
    pallas_call x1 -> x0, Pallas kernels: 1.72 us -> none  [on_device(): pl.pallas_call(functools.partial(index_kernel, 2, bus_loc), out_shape=jax...]
    unnamed x13 -> x2, local copies, waits for them, and re-layouts: 3.01 us -> 3.01 us
where the time goes in v2:
time: 38.7 us; the launch traced here: 38.5 us
  Pallas kernels  34.8 us (90%)
  local copies, waits for them, and re-layouts  3.01 us (8%)
  between operations  0.64 us (2%)
    pallas_call x1, Pallas kernels, on_device(): pl.pallas_call(main_kernel, out_shape=(jax.ShapeDtypeStruct((KS, 256), f3...  34.8 us
    unnamed x2, local copies, waits for them, and re-layouts  3.01 us

profile of v2, /device:TPU:1, one launch (start us, length us, event | category | flops | bytes accessed | tf_op | source)
XLA Modules:
  0.0 38.5 jit_solution(13544698916069119754)
XLA Ops:
  0.6 34.8 %exchange.1 = (f32[64,256]{1,0:T(8,128)}, f32[96,256]{1,0:T(8,128)}) custom-call(bf16[128,5120]{1,0:T(8,128)(2,1)} %x_hbm.1, bf16[96,5120]{1,0:T(8,128)(2,1)} %bitcast.9, s32[8,128]{1,0:T(8,128)} %bitcast.15, s32[32,128]{1,0:T(8,128)} %bitcast.12, s32[32,128]{1,0:T(8,128)} %bitcast.13, s32[16,128]{1,0:T(8,128)} %bitcast.14, f32[2,128]{1,0:T(2,128)} %bitcast.16, ...), custom_call_target="tpu_custom_call" | custom-call | tf_op jit(solution)/shard_map/exchange/pallas_call | solution.py:320
  35.5 1.5 %copy.12 = f32[256,64]{0,1:T(8,128)} copy(f32[256,64]{0,1:T(8,128)} %bitcast.11) | data formatting | bytes 131072
  36.9 1.5 %copy.13 = f32[256,96]{0,1:T(8,128)} copy(f32[256,96]{0,1:T(8,128)} %bitcast.10) | data formatting | bytes 196608

commit v3 on v2

--- a/solution.py
+++ b/solution.py
@@ -9,10 +9,9 @@
 HOURS = 12
 HPAD = 16
 KS = 64
-CHUNKS = (16, 48)
+CHUNKS = (32, 32)
 OFFS = tuple(sum(CHUNKS[:i]) for i in range(len(CHUNKS)))
-WIDTH = tuple(k + (HPAD if i == 0 else 0) for i, k in enumerate(CHUNKS))
-ROWS = tuple(2 * k + (HPAD if i == 0 else 0) for i, k in enumerate(CHUNKS))
+ROWS = tuple(2 * k for k in CHUNKS)
 NCH = len(CHUNKS)
 
 
@@ -41,10 +40,10 @@
 
 def main_kernel(
     x_hbm, inject_hbm, outage_hbm, from_hbm, to_hbm, region_hbm, susc_hbm, rating_hbm,
-    load_ref, base_ref,
+    out_ref,
     x_ref, inject_ref, outage_ref, from_ref, to_ref, region_ref, susc_ref, rating_ref, in_sem,
-    ends, efc, etc, hb, pb, ra, q, rb, p, rc, hfull, sp, rs, inc_flow, inc_sens, s4, r4,
-    s0s, s0r, s1s, s1r, s2s, s2r, s3s, s3r, shs, shr, s4s, s4r,
+    ends, efc, etc, hb, rh, ph, rch, hfull, pb, ra, q, rb, p, rc, sp, rs, inc_flow, inc_sens, s4, r4,
+    h1s, h1r, h2s, h2r, h3s, h3r, s0s, s0r, s1s, s1r, s2s, s2r, s3s, s3r, s4s, s4r,
 ):
     b = lax.axis_index("bus")
     l = lax.axis_index("line")
@@ -56,8 +55,8 @@
     loads = [
         pltpu.make_async_copy(src, dst, in_sem.at[i])
         for i, (src, dst) in enumerate((
-            (outage_hbm, outage_ref), (from_hbm, from_ref), (to_hbm, to_ref), (region_hbm, region_ref),
-            (x_hbm, x_ref), (inject_hbm, inject_ref), (susc_hbm, susc_ref), (rating_hbm, rating_ref),
+            (x_hbm, x_ref), (inject_hbm, inject_ref), (outage_hbm, outage_ref), (from_hbm, from_ref),
+            (to_hbm, to_ref), (region_hbm, region_ref), (susc_hbm, susc_ref), (rating_hbm, rating_ref),
         ))
     ]
     for load in loads:
@@ -77,7 +76,59 @@
     for dy in range(1, 4):
         pl.semaphore_signal(barrier, 1, device_id=at(zh, x, c, (y + dy) % 4, zl), device_id_type=MESH)
 
-    for load in loads[:4]:
+    started = []
+
+    def start(src, dst, ss, rs_, where):
+        copy = pltpu.make_async_remote_copy(
+            src_ref=src, dst_ref=dst, send_sem=ss, recv_sem=rs_, device_id=where, device_id_type=MESH
+        )
+        copy.start()
+        started.append(copy)
+
+    def arrived(src, dst, ss, rs_):
+        pltpu.make_async_remote_copy(
+            src_ref=src, dst_ref=dst, send_sem=ss, recv_sem=rs_,
+            device_id=at(zh, x, 1 - c, y, zl), device_id_type=MESH,
+        ).wait_recv()
+
+    for load in loads[:2]:
+        load.wait()
+    spread = lax.dot_general(
+        inject_ref[...], x_ref[...], (((1,), (1,)), ((), ())), preferred_element_type=jnp.float32
+    )
+    zero4 = jnp.zeros((HPAD - HOURS, 128), jnp.float32)
+    for xd in range(4):
+        for cd in range(2):
+            first = (xd * 2 + cd) * HOURS
+            hb[cd, xd] = jnp.concatenate([spread[first : first + HOURS], zero4], axis=0)
+
+    pl.semaphore_wait(barrier, 17)
+    for i, (gx, gc) in enumerate(group):
+        start(hb.at[gc, gx], rh.at[x * 2 + c], h1s.at[i], h1r.at[i], at(zh, gx, gc, y, zl))
+
+    def hours2():
+        rh[x * 2 + c] = hb[c, x]
+        for i in range(7):
+            fx, fc = (x + 4 - (i + 1) // 2) % 4, (c + (i + 1) % 2) % 2
+            arrived(hb.at[0, 0], rh.at[fx * 2 + fc], h1s.at[i], h1r.at[i])
+        total = ((rh[0] + rh[1]) + (rh[2] + rh[3])) + ((rh[4] + rh[5]) + (rh[6] + rh[7]))
+        mine = jnp.where(zh == 0, 1.0, 0.0) * susc_ref[...]
+        ph[...] = jnp.concatenate([total[0:HOURS], mine, jnp.zeros((2, 128), jnp.float32)], axis=0)
+        for dz in (4, 3, 5, 2, 6, 1, 7):
+            pz = (z + dz) % 8
+            start(ph, rch.at[z], h2s.at[dz], h2r.at[dz], at(pz // 4, x, c, y, pz % 4))
+
+    def hours3():
+        rch[z] = ph[...]
+        for dz in (1, 7, 2, 6, 3, 5, 4):
+            fz = (z + 8 - dz) % 8
+            arrived(ph, rch.at[fz], h2s.at[dz], h2r.at[dz])
+        hfull[y] = rch[0:4] + rch[4:8]
+        for dy in (2, 1, 3):
+            py = (y + dy) % 4
+            start(hfull.at[y], hfull.at[y], h3s.at[dy], h3r.at[dy], at(zh, x, c, py, zl))
+
+    for load in loads[2:]:
         load.wait()
     rf = lookup(from_ref, 32, outage_ref[...])
     rt = lookup(to_ref, 32, outage_ref[...])
@@ -92,17 +143,6 @@
     for s in range(8):
         efc[s] = (jnp.broadcast_to(bus_from[s : s + 1, :], (128, 128)).T - lane).astype(jnp.int16)
         etc[s] = (jnp.broadcast_to(bus_to[s : s + 1, :], (128, 128)).T - lane).astype(jnp.int16)
-
-    for load in loads[4:]:
-        load.wait()
-    spread = lax.dot_general(
-        inject_ref[...], x_ref[...], (((1,), (1,)), ((), ())), preferred_element_type=jnp.float32
-    )
-    zero4 = jnp.zeros((HPAD - HOURS, 128), jnp.float32)
-    for xd in range(4):
-        for cd in range(2):
-            first = (xd * 2 + cd) * HOURS
-            hb[cd, xd] = jnp.concatenate([spread[first : first + HOURS], zero4], axis=0)
 
     one = jnp.bfloat16(1.0)
     minus = jnp.bfloat16(-1.0)
@@ -126,24 +166,6 @@
             )
         for xd in range(4):
             pb[ch][cd, xd, 0 : 2 * k, :] = acc[xd * 2 * k : (xd + 1) * 2 * k]
-        if ch == 0:
-            for xd in range(4):
-                pb[ch][cd, xd, 2 * k : 2 * k + HPAD, :] = hb[cd, xd]
-
-    started = []
-
-    def start(src, dst, ss, rs_, where):
-        copy = pltpu.make_async_remote_copy(
-            src_ref=src, dst_ref=dst, send_sem=ss, recv_sem=rs_, device_id=where, device_id_type=MESH
-        )
-        copy.start()
-        started.append(copy)
-
-    def arrived(src, dst, ss, rs_):
-        pltpu.make_async_remote_copy(
-            src_ref=src, dst_ref=dst, send_sem=ss, recv_sem=rs_,
-            device_id=at(zh, x, 1 - c, y, zl), device_id_type=MESH,
-        ).wait_recv()
 
     def send0(ch):
         start(pb[ch].at[1 - c], ra[ch], s0s.at[ch], s0r.at[ch], at(zh, x, 1 - c, y, zl))
@@ -164,13 +186,6 @@
         total = (rb[ch][0] + rb[ch][1]) + (rb[ch][2] + rb[ch][3])
         for zd in range(2):
             p[ch][zd, 0:k, :] = total[zd * k : (zd + 1) * k]
-        if ch == 0:
-            mine = jnp.where(zh == 0, 1.0, 0.0) * susc_ref[...]
-            tail = jnp.concatenate(
-                [total[2 * k : 2 * k + HOURS], mine, jnp.zeros((2, 128), jnp.float32)], axis=0
-            )
-            for zd in range(2):
-                p[ch][zd, k : k + HPAD, :] = tail
         for dz in (4, 3, 5, 2, 6, 1, 7):
             pz = (z + dz) % 8
             start(p[ch].at[pz // 4], rc[ch].at[z], s2s.at[ch, dz], s2r.at[ch, dz], at(pz // 4, x, c, y, pz % 4))
@@ -181,11 +196,6 @@
         for dz in (1, 7, 2, 6, 3, 5, 4):
             fz = (z + 8 - dz) % 8
             arrived(p[ch].at[0], rc[ch].at[fz], s2s.at[ch, dz], s2r.at[ch, dz])
-        if ch == 0:
-            hfull[y] = rc[ch][0:4, k : k + HPAD, :] + rc[ch][4:8, k : k + HPAD, :]
-            for dy in (2, 1, 3):
-                py = (y + dy) % 4
-                start(hfull.at[y], hfull.at[y], shs.at[dy], shr.at[dy], at(zh, x, c, py, zl))
         rows = three(jnp.concatenate([rc[ch][i, 0:k, :] + rc[ch][4 + i, 0:k, :] for i in range(4)], axis=1))
         part = dot3(rows, inc_sens[...], k)
         for py in range(4):
@@ -219,35 +229,39 @@
             )
 
     select(0, 1 - c)
-    pl.semaphore_wait(barrier, 17)
     send0(0)
     select(0, c)
     send1(0)
     for ch in range(1, NCH):
         select(ch, 1 - c)
         send0(ch)
+        if ch == 1:
+            hours2()
         select(ch, c)
         send1(ch)
+    if NCH == 1:
+        hours2()
 
     for g in range(8):
         at_line = (g // 2 * 4 + zl) * 2 + g % 2
         fill(inc_sens, g, 4, from_ref[pl.ds(at_line, 1), :], to_ref[pl.ds(at_line, 1), :], y * 512)
     at_tile = zh * 4 + x
     fill(inc_sens, 8, 4, ends[0, pl.ds(at_tile, 1), :], ends[1, pl.ds(at_tile, 1), :], y * 512)
-    send2(0)
     for g in range(2):
         fill(inc_flow, g, 16, from_ref[pl.ds(l * 2 + g, 1), :], to_ref[pl.ds(l * 2 + g, 1), :], 0)
     for g in range(4):
         fill(inc_flow, 2 + g, 16, ends[0, pl.ds(zh * 4 + g, 1), :], ends[1, pl.ds(zh * 4 + g, 1), :], 0)
+    send2(0)
+    hours3()
     for ch in range(1, NCH):
         send2(ch)
-    for ch in range(NCH):
+    for ch in range(NCH - 1):
         send3(ch)
 
     susc_row = jnp.concatenate([susc_ref[0:1, :], susc_ref[1:2, :]], axis=1)
     for dy in (1, 3, 2):
         fy = (y + 4 - dy) % 4
-        arrived(hfull.at[y], hfull.at[fy], shs.at[dy], shr.at[dy])
+        arrived(hfull.at[y], hfull.at[fy], h3s.at[dy], h3r.at[dy])
     hours = jnp.concatenate([hfull[i // 4, i % 4] for i in range(16)], axis=1)
     flows = dot3(three(hours), inc_flow[...], HPAD)
     own_flow = flows[:, 0:256] * susc_row
@@ -257,6 +271,7 @@
     for i, (gx, gc) in enumerate(group):
         start(s4.at[gx], r4.at[x * 2 + c], s4s.at[i], s4r.at[i], at(zh, gx, gc, y, zl))
     r4[x * 2 + c] = s4[x]
+    send3(NCH - 1)
 
     row = outage_ref[pl.ds(at_tile, 1), :]
     table = jnp.concatenate([hfull[i // 4, i % 4, HOURS : HOURS + 2, :] for i in range(16)], axis=0)
@@ -297,12 +312,24 @@
             flow = r4[s, h : h + 1, 0:256]
             col = outflow[:, s * HPAD + h : s * HPAD + h + 1]
             worst = jnp.maximum(worst, jnp.abs(flow + ratio * col))
-    load_ref[...] = worst / jnp.concatenate([rating_ref[0:1, :], rating_ref[1:2, :]], axis=1)
+    out_ref[0:KS, :] = worst / jnp.concatenate([rating_ref[0:1, :], rating_ref[1:2, :]], axis=1)
     for s in range(8):
-        base_ref[s * HOURS : (s + 1) * HOURS, :] = r4[s, 0:HOURS, 0:256]
+        out_ref[KS + s * HOURS : KS + (s + 1) * HOURS, :] = r4[s, 0:HOURS, 0:256]
 
     for copy in started:
         copy.wait_send()
+
+
+def split_kernel(both_ref, load_ref, base_ref, here, sem):
+    load = pltpu.make_async_copy(both_ref, here, sem.at[2])
+    load.start()
+    load.wait()
+    first = pltpu.make_async_copy(here.at[0:KS, :], load_ref, sem.at[0])
+    second = pltpu.make_async_copy(here.at[KS : KS + 96, :], base_ref, sem.at[1])
+    first.start()
+    second.start()
+    first.wait()
+    second.wait()
 
 
 def on_device(xrows, inject, line_from, line_to, suscept, rating, region_bus, outage):
@@ -317,11 +344,11 @@
         region_bus.reshape(16, 128), suscept.reshape(2, 128), rating.reshape(2, 128),
     )
     sens_rows = tuple(k + 8 for k in CHUNKS)
-    load_t, base_t = pl.pallas_call(
+    both = pl.pallas_call(
         main_kernel,
-        out_shape=(jax.ShapeDtypeStruct((KS, 256), f32), jax.ShapeDtypeStruct((96, 256), f32)),
+        out_shape=jax.ShapeDtypeStruct((KS + 96, 256), f32),
         in_specs=[far] * 8,
-        out_specs=(vm, vm),
+        out_specs=vm,
         scratch_shapes=[
             *[vmem(a.shape, a.dtype) for a in args],
             sems(8),
@@ -329,24 +356,29 @@
             vmem((8, 128, 128), i16),
             vmem((8, 128, 128), i16),
             vmem((2, 4, HPAD, 128)),
+            vmem((8, HPAD, 128)),
+            vmem((HPAD, 128)),
+            vmem((8, HPAD, 128)),
+            vmem((4, 4, HPAD, 128)),
             each((2, 4), ROWS),
             each((4,), ROWS),
             each((4,), ROWS),
             each((4,), ROWS),
-            each((2,), WIDTH),
-            each((8,), WIDTH),
-            vmem((4, 4, HPAD, 128)),
+            each((2,), CHUNKS),
+            each((8,), CHUNKS),
             each((4,), sens_rows, 256),
             each((4,), sens_rows, 256),
             vmem((2048, 768), bf16),
             vmem((512, 1152), bf16),
             vmem((4, HPAD, 384)),
             vmem((8, HPAD, 384)),
+            sems(7), sems(7),
+            sems(8), sems(8),
+            sems(4), sems(4),
             sems(NCH), sems(NCH),
             sems(NCH, 4), sems(NCH, 4),
             sems(NCH, 8), sems(NCH, 8),
             sems(NCH, 4), sems(NCH, 4),
-            sems(4), sems(4),
             sems(7), sems(7),
         ],
         compiler_params=pltpu.CompilerParams(
@@ -354,6 +386,14 @@
         ),
         name="exchange",
     )(*args)
+    load_t, base_t = pl.pallas_call(
+        split_kernel,
+        out_shape=(jax.ShapeDtypeStruct((KS, 256), f32), jax.ShapeDtypeStruct((96, 256), f32)),
+        in_specs=[far],
+        out_specs=(far, far),
+        scratch_shapes=[vmem((KS + 96, 256)), sems(3)],
+        name="outputs",
+    )(both)
     return load_t.T, base_t.T
 
 

time: 38.7 us -> 35 us (0.904)
  local copies, waits for them, and re-layouts: 3.01 us -> 0 us
  Pallas kernels: 34.8 us -> 34.2 us
    unnamed x2 -> x0, local copies, waits for them, and re-layouts: 3.01 us -> none
    pallas_call x1 -> x2, Pallas kernels: 34.8 us -> 34.2 us  [the longest x1 32.6 us: on_device(): pl.pallas_call(main_kernel, out_shape=jax.ShapeDtypeStruct((KS + 96, 256)...]
where the time goes in v3:
time: 35 us; the launch traced here: 34.9 us
  Pallas kernels  34.2 us (98%)
  between operations  0.64 us (2%)
    pallas_call x1, Pallas kernels, on_device(): pl.pallas_call(main_kernel, out_shape=jax.ShapeDtypeStruct((KS + 96, 256)...  32.6 us
    pallas_call x1, Pallas kernels, on_device(): pl.pallas_call(split_kernel, out_shape=(jax.ShapeDtypeStruct((KS, 256), f...  1.6 us

profile of v3, /device:TPU:1, one launch (start us, length us, event | category | flops | bytes accessed | tf_op | source)
XLA Modules:
  0.0 34.9 jit_solution(7047811347606695777)
XLA Ops:
  0.6 32.6 %exchange.1.both_ref = f32[160,256]{1,0:T(8,128)} custom-call(bf16[128,5120]{1,0:T(8,128)(2,1)} %x_hbm.1, bf16[96,5120]{1,0:T(8,128)(2,1)} %bitcast.9, s32[8,128]{1,0:T(8,128)} %bitcast.13, s32[32,128]{1,0:T(8,128)} %bitcast.10, s32[32,128]{1,0:T(8,128)} %bitcast.11, s32[16,128]{1,0:T(8,128)} %bitcast.12, f32[2,128]{1,0:T(2,128)} %bitcast.14, f32[2,128]{1,0:T(2,128)} %bitcast.15), custom_call_target="tpu_custom_call" | custom-call | tf_op jit(solution)/shard_map/exchange/pallas_call | solution.py:347
  33.3 1.6 %outputs.1 = (f32[64,256]{1,0:T(8,128)}, f32[96,256]{1,0:T(8,128)}) custom-call(f32[160,256]{1,0:T(8,128)} %exchange.1.both_ref), custom_call_target="tpu_custom_call" | custom-call | tf_op jit(solution)/shard_map/outputs/pallas_call | solution.py:389

commit v4 on v3

--- a/solution.py
+++ b/solution.py
@@ -91,6 +91,22 @@
             device_id=at(zh, x, 1 - c, y, zl), device_id_type=MESH,
         ).wait_recv()
 
+    for load in loads[2:]:
+        load.wait()
+    rf = lookup(from_ref, 32, outage_ref[...])
+    rt = lookup(to_ref, 32, outage_ref[...])
+    ends[0] = rf
+    ends[1] = rt
+    bus_from = lookup(region_ref, 16, rf) - b * bus_loc
+    bus_to = lookup(region_ref, 16, rt) - b * bus_loc
+    bus_from = jnp.where((bus_from >= 0) & (bus_from < bus_loc), bus_from, -512)
+    bus_to = jnp.where((bus_to >= 0) & (bus_to < bus_loc), bus_to, -512)
+
+    lane = lax.broadcasted_iota(jnp.int32, (128, 128), 1)
+    for s in range(8):
+        efc[s] = (jnp.broadcast_to(bus_from[s : s + 1, :], (128, 128)).T - lane).astype(jnp.int16)
+        etc[s] = (jnp.broadcast_to(bus_to[s : s + 1, :], (128, 128)).T - lane).astype(jnp.int16)
+
     for load in loads[:2]:
         load.wait()
     spread = lax.dot_general(
@@ -102,9 +118,6 @@
             first = (xd * 2 + cd) * HOURS
             hb[cd, xd] = jnp.concatenate([spread[first : first + HOURS], zero4], axis=0)
 
-    pl.semaphore_wait(barrier, 17)
-    for i, (gx, gc) in enumerate(group):
-        start(hb.at[gc, gx], rh.at[x * 2 + c], h1s.at[i], h1r.at[i], at(zh, gx, gc, y, zl))
 
     def hours2():
         rh[x * 2 + c] = hb[c, x]
@@ -127,22 +140,6 @@
         for dy in (2, 1, 3):
             py = (y + dy) % 4
             start(hfull.at[y], hfull.at[y], h3s.at[dy], h3r.at[dy], at(zh, x, c, py, zl))
-
-    for load in loads[2:]:
-        load.wait()
-    rf = lookup(from_ref, 32, outage_ref[...])
-    rt = lookup(to_ref, 32, outage_ref[...])
-    ends[0] = rf
-    ends[1] = rt
-    bus_from = lookup(region_ref, 16, rf) - b * bus_loc
-    bus_to = lookup(region_ref, 16, rt) - b * bus_loc
-    bus_from = jnp.where((bus_from >= 0) & (bus_from < bus_loc), bus_from, -512)
-    bus_to = jnp.where((bus_to >= 0) & (bus_to < bus_loc), bus_to, -512)
-
-    lane = lax.broadcasted_iota(jnp.int32, (128, 128), 1)
-    for s in range(8):
-        efc[s] = (jnp.broadcast_to(bus_from[s : s + 1, :], (128, 128)).T - lane).astype(jnp.int16)
-        etc[s] = (jnp.broadcast_to(bus_to[s : s + 1, :], (128, 128)).T - lane).astype(jnp.int16)
 
     one = jnp.bfloat16(1.0)
     minus = jnp.bfloat16(-1.0)
@@ -229,7 +226,10 @@
             )
 
     select(0, 1 - c)
+    pl.semaphore_wait(barrier, 17)
     send0(0)
+    for i, (gx, gc) in enumerate(group):
+        start(hb.at[gc, gx], rh.at[x * 2 + c], h1s.at[i], h1r.at[i], at(zh, gx, gc, y, zl))
     select(0, c)
     send1(0)
     for ch in range(1, NCH):
@@ -247,11 +247,11 @@
         fill(inc_sens, g, 4, from_ref[pl.ds(at_line, 1), :], to_ref[pl.ds(at_line, 1), :], y * 512)
     at_tile = zh * 4 + x
     fill(inc_sens, 8, 4, ends[0, pl.ds(at_tile, 1), :], ends[1, pl.ds(at_tile, 1), :], y * 512)
+    send2(0)
     for g in range(2):
         fill(inc_flow, g, 16, from_ref[pl.ds(l * 2 + g, 1), :], to_ref[pl.ds(l * 2 + g, 1), :], 0)
     for g in range(4):
         fill(inc_flow, 2 + g, 16, ends[0, pl.ds(zh * 4 + g, 1), :], ends[1, pl.ds(zh * 4 + g, 1), :], 0)
-    send2(0)
     hours3()
     for ch in range(1, NCH):
         send2(ch)
@@ -283,38 +283,35 @@
         jnp.where(high == lax.broadcasted_iota(jnp.int32, (32, 128), 0), cand, 0.0), axis=0, keepdims=True
     )
 
-    sens = []
-    own = jnp.zeros((1, 128), jnp.float32)
+    for i in range(7):
+        fx, fc = (x + 4 - (i + 1) // 2) % 4, (c + (i + 1) % 2) % 2
+        arrived(s4.at[0], r4.at[fx * 2 + fc], s4s.at[i], s4r.at[i])
+    outflow = r4[:, :, 256:384].reshape(128, 128) * susc_out
+    outflow = outflow.T
+    outflow = jnp.where(c == 0, outflow[0:KS], outflow[KS : 2 * KS])
+    rating_row = jnp.concatenate([rating_ref[0:1, :], rating_ref[1:2, :]], axis=1)
+    for s in range(8):
+        out_ref[KS + s * HOURS : KS + (s + 1) * HOURS, :] = r4[s, 0:HOURS, 0:256]
     for ch in range(NCH):
-        k = CHUNKS[ch]
+        k, first = CHUNKS[ch], OFFS[ch]
         for dy in (1, 3, 2):
             fy = (y + 4 - dy) % 4
             arrived(sp[ch].at[0], rs[ch].at[fy], s3s.at[ch, dy], s3r.at[ch, dy])
         total = (rs[ch][0] + rs[ch][1]) + (rs[ch][2] + rs[ch][3])
-        sens.append(total[0:k])
-        own = own + total[k : k + 1, 0:128]
-    sens = jnp.concatenate(sens, axis=0) * susc_row
-    here = lax.broadcasted_iota(jnp.int32, (KS, 128), 1) == lax.broadcasted_iota(jnp.int32, (KS, 128), 0) + c * KS
-    divisor = jnp.maximum(1.0 - own * susc_out, 0.25)
-    divisor = jnp.sum(jnp.where(here, jnp.broadcast_to(divisor, (KS, 128)), 0.0), axis=1, keepdims=True)
-    ratio = sens / divisor
-
-    for i in range(7):
-        fx, fc = (x + 4 - (i + 1) // 2) % 4, (c + (i + 1) % 2) % 2
-        arrived(s4.at[0], r4.at[fx * 2 + fc], s4s.at[i], s4r.at[i])
-
-    outflow = r4[:, :, 256:384].reshape(128, 128) * susc_out
-    outflow = outflow.T
-    outflow = jnp.where(c == 0, outflow[0:KS], outflow[KS : 2 * KS])
-    worst = jnp.zeros((KS, 256), jnp.float32)
-    for s in range(8):
-        for h in range(HOURS):
-            flow = r4[s, h : h + 1, 0:256]
-            col = outflow[:, s * HPAD + h : s * HPAD + h + 1]
-            worst = jnp.maximum(worst, jnp.abs(flow + ratio * col))
-    out_ref[0:KS, :] = worst / jnp.concatenate([rating_ref[0:1, :], rating_ref[1:2, :]], axis=1)
-    for s in range(8):
-        out_ref[KS + s * HOURS : KS + (s + 1) * HOURS, :] = r4[s, 0:HOURS, 0:256]
+        divisor = jnp.maximum(1.0 - total[k : k + 1, 0:128] * susc_out, 0.25)
+        here = (
+            lax.broadcasted_iota(jnp.int32, (k, 128), 1)
+            == lax.broadcasted_iota(jnp.int32, (k, 128), 0) + (c * KS + first)
+        )
+        divisor = jnp.sum(jnp.where(here, jnp.broadcast_to(divisor, (k, 128)), 0.0), axis=1, keepdims=True)
+        ratio = total[0:k] * susc_row / divisor
+        worst = jnp.zeros((k, 256), jnp.float32)
+        for s in range(8):
+            for h in range(HOURS):
+                flow = r4[s, h : h + 1, 0:256]
+                col = outflow[first : first + k, s * HPAD + h : s * HPAD + h + 1]
+                worst = jnp.maximum(worst, jnp.abs(flow + ratio * col))
+        out_ref[first : first + k, :] = worst / rating_row
 
     for copy in started:
         copy.wait_send()

time: 35 us -> 33.9 us (0.969)
  Pallas kernels: 34.2 us -> 33.1 us
    pallas_call x1, Pallas kernels: 32.6 us -> 31.5 us  [on_device(): pl.pallas_call(main_kernel, out_shape=jax.ShapeDtypeStruct((KS + 96, 256)...]
where the time goes in v4:
time: 33.9 us; the launch traced here: 33.8 us
  Pallas kernels  33.1 us (98%)
  between operations  0.64 us (2%)
    pallas_call x1, Pallas kernels, on_device(): pl.pallas_call(main_kernel, out_shape=jax.ShapeDtypeStruct((KS + 96, 256)...  31.5 us
    pallas_call x1, Pallas kernels, on_device(): pl.pallas_call(split_kernel, out_shape=(jax.ShapeDtypeStruct((KS, 256), f...  1.6 us

profile of v4, /device:TPU:1, one launch (start us, length us, event | category | flops | bytes accessed | tf_op | source)
XLA Modules:
  0.0 33.8 jit_solution(3048692585306109656)
XLA Ops:
  0.6 31.5 %exchange.1.both_ref = f32[160,256]{1,0:T(8,128)} custom-call(bf16[128,5120]{1,0:T(8,128)(2,1)} %x_hbm.1, bf16[96,5120]{1,0:T(8,128)(2,1)} %bitcast.9, s32[8,128]{1,0:T(8,128)} %bitcast.13, s32[32,128]{1,0:T(8,128)} %bitcast.10, s32[32,128]{1,0:T(8,128)} %bitcast.11, s32[16,128]{1,0:T(8,128)} %bitcast.12, f32[2,128]{1,0:T(2,128)} %bitcast.14, f32[2,128]{1,0:T(2,128)} %bitcast.15), custom_call_target="tpu_custom_call" | custom-call | tf_op jit(solution)/shard_map/exchange/pallas_call | solution.py:344
  32.2 1.6 %outputs.1 = (f32[64,256]{1,0:T(8,128)}, f32[96,256]{1,0:T(8,128)}) custom-call(f32[160,256]{1,0:T(8,128)} %exchange.1.both_ref), custom_call_target="tpu_custom_call" | custom-call | tf_op jit(solution)/shard_map/outputs/pallas_call | solution.py:386

commit v5 on v4

--- a/solution.py
+++ b/solution.py
@@ -40,8 +40,8 @@
 
 def main_kernel(
     x_hbm, inject_hbm, outage_hbm, from_hbm, to_hbm, region_hbm, susc_hbm, rating_hbm,
-    out_ref,
-    x_ref, inject_ref, outage_ref, from_ref, to_ref, region_ref, susc_ref, rating_ref, in_sem,
+    out_hbm,
+    x_ref, inject_ref, outage_ref, from_ref, to_ref, region_ref, susc_ref, rating_ref, in_sem, out_ref, out_sem,
     ends, efc, etc, hb, rh, ph, rch, hfull, pb, ra, q, rb, p, rc, sp, rs, inc_flow, inc_sens, s4, r4,
     h1s, h1r, h2s, h2r, h3s, h3r, s0s, s0r, s1s, s1r, s2s, s2r, s3s, s3r, s4s, s4r,
 ):
@@ -292,6 +292,8 @@
     rating_row = jnp.concatenate([rating_ref[0:1, :], rating_ref[1:2, :]], axis=1)
     for s in range(8):
         out_ref[KS + s * HOURS : KS + (s + 1) * HOURS, :] = r4[s, 0:HOURS, 0:256]
+    stores = [pltpu.make_async_copy(out_ref.at[KS : KS + 96, :], out_hbm.at[KS : KS + 96, :], out_sem.at[NCH])]
+    stores[0].start()
     for ch in range(NCH):
         k, first = CHUNKS[ch], OFFS[ch]
         for dy in (1, 3, 2):
@@ -312,9 +314,14 @@
                 col = outflow[first : first + k, s * HPAD + h : s * HPAD + h + 1]
                 worst = jnp.maximum(worst, jnp.abs(flow + ratio * col))
         out_ref[first : first + k, :] = worst / rating_row
+        rows = pl.ds(first, k)
+        stores.append(pltpu.make_async_copy(out_ref.at[rows, :], out_hbm.at[rows, :], out_sem.at[ch]))
+        stores[-1].start()
 
     for copy in started:
         copy.wait_send()
+    for store in stores:
+        store.wait()
 
 
 def split_kernel(both_ref, load_ref, base_ref, here, sem):
@@ -330,7 +337,6 @@
 
 
 def on_device(xrows, inject, line_from, line_to, suscept, rating, region_bus, outage):
-    vm = pl.BlockSpec(memory_space=pltpu.VMEM)
     far = pl.BlockSpec(memory_space=pl.ANY)
     f32, bf16, i16, i32 = jnp.float32, jnp.bfloat16, jnp.int16, jnp.int32
     vmem = lambda shape, kind=f32: pltpu.VMEM(shape, kind)
@@ -345,10 +351,12 @@
         main_kernel,
         out_shape=jax.ShapeDtypeStruct((KS + 96, 256), f32),
         in_specs=[far] * 8,
-        out_specs=vm,
+        out_specs=far,
         scratch_shapes=[
             *[vmem(a.shape, a.dtype) for a in args],
             sems(8),
+            vmem((KS + 96, 256)),
+            sems(NCH + 1),
             vmem((2, 8, 128), i32),
             vmem((8, 128, 128), i16),
             vmem((8, 128, 128), i16),

time: 33.9 us -> 33.8 us (level)
  no operation moved by 1% of the time
where the time goes in v5:
time: 33.8 us; the launch traced here: 33.6 us
  Pallas kernels  33 us (98%)
  between operations  0.64 us (2%)
    pallas_call x1, Pallas kernels, on_device(): pl.pallas_call(main_kernel, out_shape=jax.ShapeDtypeStruct((KS + 96, 256)...  31.4 us
    pallas_call x1, Pallas kernels, on_device(): pl.pallas_call(split_kernel, out_shape=(jax.ShapeDtypeStruct((KS, 256), f...  1.6 us

profile of v5, /device:TPU:1, one launch (start us, length us, event | category | flops | bytes accessed | tf_op | source)
XLA Modules:
  0.0 33.6 jit_solution(2065702144644839034)
XLA Ops:
  0.6 31.4 %exchange.1.both_ref = f32[160,256]{1,0:T(8,128)} custom-call(bf16[128,5120]{1,0:T(8,128)(2,1)} %x_hbm.1, bf16[96,5120]{1,0:T(8,128)(2,1)} %bitcast.9, s32[8,128]{1,0:T(8,128)} %bitcast.13, s32[32,128]{1,0:T(8,128)} %bitcast.10, s32[32,128]{1,0:T(8,128)} %bitcast.11, s32[16,128]{1,0:T(8,128)} %bitcast.12, f32[2,128]{1,0:T(2,128)} %bitcast.14, f32[2,128]{1,0:T(2,128)} %bitcast.15), custom_call_target="tpu_custom_call" | custom-call | tf_op jit(solution)/shard_map/exchange/pallas_call | solution.py:350
  32.0 1.6 %outputs.1 = (f32[64,256]{1,0:T(8,128)}, f32[96,256]{1,0:T(8,128)}) custom-call(f32[160,256]{1,0:T(8,128)} %exchange.1.both_ref), custom_call_target="tpu_custom_call" | custom-call | tf_op jit(solution)/shard_map/outputs/pallas_call | solution.py:394
